TPU v7x, 32 devices: a whole 2x2x4 slice. The times are simulated.
32 devices in a mesh: groups: 2 (over x), dp: 8 (over z, y), mp: 2 (over core).
Axes of the slice: x: 2, y: 2, z: 4, core: 2. Of those that a mesh axis runs over, the one named last changes fastest.
Arguments:
- residual: bfloat16 [256, 4096], P(('groups', 'dp')), parts along dimension 0, may hold values from -40 to 40
- queries: bfloat16 [256, 2048], P(('groups', 'dp'), 'mp'), parts along dimension 0, may hold values from -27 to 27
- new_kv: bfloat16 [256, 2, 2048], P(('groups', 'dp'), None, 'mp'), parts along dimension 0, may hold values from -6 to 6
- kv_pool: bfloat16 [960, 2, 16, 2048], P(('groups', 'dp'), None, None, 'mp'), parts along dimension 0, may hold values from -6 to 6
- cache_len: int32 [256], P(('groups', 'dp')), parts along dimension 0, may hold values from 24 to 47, as said below
- reconnect: int32 [64, 5], P('groups'), parts along dimension 0, may hold values from 0 to 127, as said below
- audio_tokens: int32 [256, 8], P(('groups', 'dp', 'mp')), parts along dimension 0, may hold values from 0 to 1023
- out_weight: bfloat16 [2048, 4096], P('mp'), may hold values from -0.125 to 0.125
- norm_gain: float32 [4096], replicated, may hold values from 0.1 to 1.9
- depth_in: bfloat16 [4096, 1024], P('mp'), may hold values from -0.09375 to 0.09375
- code_embed: bfloat16 [1024, 1024], replicated, may hold values from -6 to 6
- depth_gain: float32 [1024], replicated, may hold values from 0.1 to 1.9
- depth_head: bfloat16 [1024, 1024], replicated, may hold values from -0.1875 to 0.1875
Outputs:
- logits: bfloat16 [256, 8, 1024], P(('groups', 'dp', 'mp')), parts along dimension 0
- new_cache: bfloat16 [768, 2, 16, 2048], P(('groups', 'dp'), None, None, 'mp'), parts along dimension 0
There are 2 independent parts, one for each index of `groups`. A program takes and returns all parts, laid end to end along the dimension named above; an argument that names none is the same for every part. Nothing has to cross between parts.
Inputs may be any that keep to these rules, and one draw needn't show every extreme that they name: `cache_len`: between 24 and 47; in each block of 16 sessions one session has 47 unless reset by a reconnect entry, and each holder's first listed session has 47. `reconnect`: row r: session, holding index of dp, owner index of dp (session // 16), page count ceil(cache_len of the session / 16) (up to 3, reached at every holder), first pool page local to the holder, equal to 48 + k * 3 for the holder's k-th entry. Holder differs from owner; each holder lists 4 sessions of distinct owners; a session appears at most once.
All inputs are finite; a program needn't handle non-finite values.
Results may differ from a plain program's by a relative error of at most 0.006.
Values may be sent and summed in bfloat16 or wider, within the bound.
A program may use at most 128 MiB of HBM per device.

v0:
```python
import jax
import jax.numpy as jnp
from jax import lax
from jax.sharding import PartitionSpec as P

HD = 128
PAGES = 3


def attend(queries, kv_pages, lengths):
    batch_size, page_count, _, page_size, feature_width = kv_pages.shape
    head_count = feature_width // HD
    context_span = page_count * page_size
    key_rows = kv_pages[:, :, 0].reshape(batch_size, context_span, head_count, HD)
    value_rows = kv_pages[:, :, 1].reshape(batch_size, context_span, head_count, HD)
    query_heads = queries.reshape(batch_size, head_count, HD)
    scores = jnp.einsum(
        "bhd,bthd->bht", query_heads, key_rows, preferred_element_type=jnp.float32
    ) * HD ** (-0.5)
    position = jnp.arange(context_span, dtype=jnp.int32)
    visible = position[None, None, :] <= lengths[:, None, None]
    highest = jnp.max(jnp.where(visible, scores, -jnp.inf), -1, keepdims=True)
    weights = jnp.where(visible, jnp.exp(scores - highest), 0.0)
    weights = (weights / jnp.sum(weights, -1, keepdims=True)).astype(jnp.bfloat16)
    mixture = jnp.einsum("bht,bthd->bhd", weights, value_rows, preferred_element_type=jnp.float32)
    return mixture.reshape(batch_size, feature_width).astype(jnp.bfloat16)


def write_new(kv_pages, new_kv, lengths):
    page_count, page_size = (kv_pages.shape[1], kv_pages.shape[3])
    position = (
        jnp.arange(page_count, dtype=jnp.int32)[:, None] * page_size
        + jnp.arange(page_size, dtype=jnp.int32)[None, :]
    )
    landed = position[None, :, :] == lengths[:, None, None]
    return jnp.where(landed[:, :, None, :, None], new_kv[:, None, :, None, :], kv_pages)


def on_device(
    residual,
    queries,
    new_kv,
    kv_pool,
    cache_len,
    reconnect,
    audio_tokens,
    out_weight,
    norm_gain,
    depth_in,
    code_embed,
    depth_gain,
    depth_head,
):
    dp_count = lax.axis_size("dp")
    dp_index = lax.axis_index("dp")
    mp_index = lax.axis_index("mp")
    per_block = queries.shape[0]
    page_ids = jnp.arange(PAGES, dtype=jnp.int32)
    owner_ids = jnp.arange(dp_count, dtype=jnp.int32)
    session_ids = dp_index * per_block + jnp.arange(per_block, dtype=jnp.int32)
    picked = (
        (reconnect[None, :, 1] == dp_index) & (reconnect[None, :, 2] == owner_ids[:, None])
    ).astype(jnp.int32)
    send_first = jnp.sum(picked * reconnect[None, :, 4], 1)
    send_total = jnp.sum(picked * reconnect[None, :, 3], 1)
    slot_ids = send_first[:, None] + page_ids[None, :]
    outbound = kv_pool[slot_ids]
    live_page = page_ids[None, :] < send_total[:, None]
    outbound = jnp.where(live_page[:, :, None, None, None], outbound, jnp.zeros((), outbound.dtype))
    inbound = lax.all_to_all(outbound, "dp", split_axis=0, concat_axis=0, tiled=True)
    matched = (session_ids[:, None] == reconnect[None, :, 0]).astype(jnp.int32)
    linked = jnp.sum(matched, 1) > 0
    holder = jnp.sum(matched * reconnect[None, :, 1], 1)
    resident = kv_pool[: per_block * PAGES].reshape((per_block, PAGES) + kv_pool.shape[1:])
    fetched = inbound[holder]
    kv_pages = jnp.where(linked[:, None, None, None, None], fetched, resident)
    kv_pages = write_new(kv_pages, new_kv, cache_len)
    new_cache = kv_pages.reshape((per_block * PAGES,) + kv_pool.shape[1:])
    attention = attend(queries, kv_pages, cache_len)
    partial_out = jnp.dot(attention, out_weight, preferred_element_type=jnp.float32)
    half_width = depth_in.shape[0]
    summed = lax.psum(partial_out, "mp")
    layer_out = (residual.astype(jnp.float32) + summed).astype(jnp.bfloat16)
    layer_out = lax.optimization_barrier(layer_out).astype(jnp.float32)
    inverse_rms = lax.rsqrt(jnp.mean(layer_out * layer_out, 1, keepdims=True) + 1e-05)
    normed = (layer_out * inverse_rms * norm_gain).astype(jnp.bfloat16)
    my_half = lax.dynamic_slice_in_dim(normed, mp_index * half_width, half_width, 1)
    lifted = jnp.dot(my_half, depth_in, preferred_element_type=jnp.float32)
    depth_input = lax.psum_scatter(lifted, "mp", scatter_dimension=0, tiled=True)
    embedded = code_embed[audio_tokens].astype(jnp.float32)
    hidden = depth_input[:, None, :] + embedded
    depth_rms = lax.rsqrt(jnp.mean(hidden * hidden, -1, keepdims=True) + 1e-05)
    depth_normed = (hidden * depth_rms * depth_gain).astype(jnp.bfloat16)
    logits = jnp.dot(
        depth_normed.reshape(-1, hidden.shape[-1]), depth_head, preferred_element_type=jnp.float32
    )
    logits = logits.astype(jnp.bfloat16).reshape(audio_tokens.shape + (depth_head.shape[1],))
    return (logits, new_cache)


def solution(mesh):
    in_specs = (
        P(("groups", "dp"), None),
        P(("groups", "dp"), "mp"),
        P(("groups", "dp"), None, "mp"),
        P(("groups", "dp"), None, None, "mp"),
        P(("groups", "dp")),
        P("groups", None),
        P(("groups", "dp", "mp"), None),
        P("mp", None),
        P(),
        P("mp", None),
        P(),
        P(),
        P(),
    )
    out_specs = (P(("groups", "dp", "mp"), None, None), P(("groups", "dp"), None, None, "mp"))
    return jax.shard_map(
        on_device, mesh=mesh, in_specs=in_specs, out_specs=out_specs, check_vma=False
    )
```

profile of v0, /device:TPU:18, one launch (start us, length us, event | category | flops | bytes accessed | tf_op | source)
XLA Modules:
  0.0 120.5 jit_solution(1860783531994698838)
XLA Ops:
  7.2 0.0 copy-start
  7.2 0.9 slice_bitcast_fusion.3
  8.1 0.7 broadcast_compare_fusion.2
  8.8 0.1 select_reduce_fusion.2
  8.9 0.1 compare_select_fusion.1
  9.0 0.1 reshape.203
  9.1 0.1 iota_compare_fusion.2
  9.2 4.0 %gather_fusion = bf16[24,2,16,1024]{3,2,1,0:T(8,128)(2,1)} fusion(bf16[60,2,16,1024]{3,2,1,0:T(8,128)(2,1)} %param.16, s32[1024]{0:T(1024)S(1)} %pad_clamp_fusion.2), kind=kCustom, calls=%fused_computation | custom fusion | bytes 3145824 | tf_op jit(solution)/shard_map/gather | solution.py:67
  13.1 2.7 %broadcast_select_fusion = bf16[8,3,2,16,1024]{4,3,2,1,0:T(8,128)(2,1)} fusion(bf16[8,3,2,16,1024]{4,3,2,1,0:T(8,128)(2,1)} %bitcast.68, pred[8,3]{1,0:T(8,128)(4,1)S(1)} %iota_compare_fusion.2), kind=kLoop, calls=%fused_computation.12 | loop fusion | flops 786432 | bytes 3145752 | tf_op jit(solution)/shard_map/jit(_where)/select_n | solution.py:69
  15.9 0.0 copy-start.5
  15.9 0.0 copy-start.4
  15.9 6.3 %all-to-all-start = ((bf16[8,3,2,16,1024]{4,3,2,1,0:T(8,128)(2,1)}), bf16[8,3,2,16,1024]{4,3,2,1,0:T(8,128)(2,1)}, u32[]{:S(2)}, u32[]{:S(2)}) async-start(bf16[8,3,2,16,1024]{4,3,2,1,0:T(8,128)(2,1)} %broadcast_select_fusion), calls=%async_computation | async-start | bytes 3145728 | tf_op jit(solution)/shard_map/all_to_all | solution.py:70
  22.2 0.0 all-reduce.2.cloned.1.call-start
  22.2 0.2 fusion.40
  22.4 0.1 broadcast_in_dim.109
  22.4 0.1 broadcast_in_dim.110
  22.5 0.1 iota_add_fusion
  22.7 0.0 copy-done.5
  22.7 0.1 eq.85
  22.7 0.1 eq.86
  22.8 0.0 copy-done.4
  22.9 0.1 iota_compare_fusion
  23.0 0.1 broadcast_compare_fusion
  23.1 0.1 broadcast_compare_fusion.1
  23.1 0.0 copy-start.2
  23.1 32.8 %all-to-all-done = bf16[8,3,2,16,1024]{4,3,2,1,0:T(8,128)(2,1)} async-done(((bf16[8,3,2,16,1024]{4,3,2,1,0:T(8,128)(2,1)}), bf16[8,3,2,16,1024]{4,3,2,1,0:T(8,128)(2,1)}, u32[]{:S(2)}, u32[]{:S(2)}) %all-to-all-start) | async-done | bytes 1572896 | tf_op jit(solution)/shard_map/all_to_all | solution.py:70
  55.9 3.8 %gather_fusion.1 = bf16[16,3,2,16,1024]{4,3,2,1,0:T(8,128)(2,1)} fusion(bf16[8,3,2,16,1024]{4,3,2,1,0:T(8,128)(2,1)} %all-to-all-done, s32[1024]{0:T(1024)S(1)} %pad_clamp_fusion.1), kind=kCustom, calls=%fused_computation.1 | custom fusion | bytes 6291520 | tf_op jit(solution)/shard_map/gather | solution.py:75
  59.7 0.0 copy-done.2
  59.7 0.1 broadcast_in_dim.106
  59.8 0.0 copy-start.1
  59.8 4.4 %fusion.2 = (bf16[48,2,16,1024]{3,2,1,0:T(8,128)(2,1)}, bf16[48,2,16,1024]{3,2,1,0:T(8,128)(2,1)S(1)}) fusion(bf16[16,3,2,16,1024]{4,3,2,1,0:T(8,128)(2,1)} %gather_fusion.1, pred[48]{0:T(512)(128)(4,1)S(1)} %broadcast_in_dim.110, pred[48,16]{1,0:T(8,128)(4,1)S(1)} %broadcast_compare_fusion.1, bf16[48,2,1024]{2,1,0:T(2,128)(2,1)S(1)} %bitcast.73, ...), kind=kLoop, calls=%fused_computation.6 | loop fusion | flops 3145728 | bytes 12780336 | tf_op jit(solution)/shard_map/jit(_where)/select_n | solution.py:36
  64.3 0.0 copy-done.1
  64.3 0.4 select_select_fusion
  64.7 0.6 fusion.47
  65.3 0.4 copy.21
  65.8 1.6 %copy.22 = bf16[96,8,8,128]{3,2,1,0:T(8,128)(2,1)} copy(bf16[96,8,8,128]{3,1,2,0:T(8,128)(2,1)S(1)} %bitcast.69) | data formatting | bytes 3145728
  67.4 0.9 fusion.5
  68.3 0.2 fusion.13
  68.5 1.9 %fusion.3 = f32[16,8,1,128]{3,2,1,0:T(1,128)S(1)} fusion(bf16[16,48,8,128]{3,2,1,0:T(8,128)(2,1)} %bitcast.71, bf16[16,8,48,1]{2,1,0,3:T(8,128)(2,1)S(1)} %fusion.13), kind=kOutput, calls=%fused_computation.8 | convolution fusion | flops 1572864 | bytes 1650688 | tf_op jit(solution)/shard_map/bht,bthd->bhd/dot_general | solution.py:25
  70.4 0.0 copy-start.7
  70.4 0.0 copy-start.3
  70.5 5.3 %fusion.34 = f32[16,4096]{1,0:T(8,128)} fusion(bf16[1024,4096]{1,0:T(8,128)(2,1)} %param.20, bf16[2,8,8,128]{3,2,1,0:T(8,128)(2,1)S(1)} %bitcast.74), kind=kOutput, calls=%fused_computation.44 | convolution fusion | flops 134217728 | bytes 8683520 | tf_op jit(solution)/shard_map/dot_general | solution.py:80
  75.8 0.0 all-reduce.2.cloned.1.call-update
  75.8 0.0 reduce-scatter.2.cloned.1.call-start
  75.9 0.0 copy-done.7
  75.9 20.5 %all-reduce.2.cloned.1.call-done = f32[16,4096]{1,0:T(8,128)} async-done(((f32[16,4096]{1,0:T(8,128)}), f32[16,4096]{1,0:T(8,128)}) %all-reduce.2.cloned.1.call-update) | async-done | bytes 262160 | tf_op jit(solution)/shard_map/psum | solution.py:82
  96.4 0.0 copy-done.3
  96.4 1.0 add_convert_fusion
  97.4 0.1 multiply_reduce_fusion
  97.5 0.0 copy-start.8
  97.5 0.0 copy-start.6
  97.6 3.5 %fusion.28 = f32[16,1024]{1,0:T(8,128)} fusion(bf16[2048,1024]{1,0:T(8,128)(2,1)} %param.22, f32[16,4096]{1,0:T(8,128)S(1)} %convert_element_type.43, s32[]{:T(128)S(6)} %select_n.58, f32[2048]{0:T(1024)S(1)} %dynamic-slice, f32[16]{0:T(128)S(1)} %add_rsqrt_fusion.1), kind=kOutput, calls=%fused_computation.39 | convolution fusion | flops 67207168 | bytes 4399620 | tf_op jit(solution)/shard_map/dot_general | solution.py:88
  101.1 0.0 reduce-scatter.2.cloned.1.call-update
  101.1 0.0 copy-done.8
  101.1 0.1 reshape.219
  101.2 0.0 copy-done
  101.2 0.7 gather_fusion.2
  101.9 7.9 %reduce-scatter.2.cloned.1.call-done = f32[8,1024]{1,0:T(8,128)} async-done(((f32[16,1024]{1,0:T(8,128)}), f32[8,1024]{1,0:T(8,128)}) %reduce-scatter.2.cloned.1.call-update) | async-done | bytes 32784 | tf_op jit(solution)/shard_map/reduce_scatter | solution.py:89
  109.9 0.9 fusion.19
  110.8 0.1 rsqrt.21
  110.8 0.0 copy-done.6
  110.8 2.8 %fusion.7 = bf16[8,8,1024]{2,1,0:T(8,128)(2,1)} fusion(bf16[1024,1024]{1,0:T(8,128)(2,1)} %param.25, bf16[64,1024]{1,0:T(8,128)(2,1)S(1)} %gather_fusion.2, f32[1024]{0:T(1024)S(1)} %copy-done.6, f32[64]{0:T(128)S(1)} %rsqrt.21, f32[8,1024]{1,0:T(8,128)} %reduce-scatter.2.cloned.1.call-done), kind=kOutput, calls=%fused_computation.14 | convolution fusion | flops 134610944 | bytes 2396416 | tf_op jit(solution)/shard_map/dot_general | solution.py:94
  (16 shorter events, 0.2 us)
Async XLA Ops:
  7.2 94.1 %copy-start = (bf16[1024,1024]{1,0:T(8,128)(2,1)S(1)}, bf16[1024,1024]{1,0:T(8,128)(2,1)}, u32[]{:S(2)}) copy-start(bf16[1024,1024]{1,0:T(8,128)(2,1)} %param.23) | copy-start | bytes 6291460
  15.9 6.8 %copy-start.5 = (s32[16]{0:T(128)S(1)}, s32[16]{0:T(128)}, u32[]{:S(2)}) copy-start(s32[16]{0:T(128)} %param.17) | copy-start | bytes 196
  15.9 7.0 %copy-start.4 = (bf16[16,1024]{1,0:T(8,128)(2,1)S(1)}, bf16[16,1024]{1,0:T(8,128)(2,1)}, u32[]{:S(2)}) copy-start(bf16[16,1024]{1,0:T(8,128)(2,1)} %param.14) | copy-start | bytes 98308
  15.9 40.0 %all-to-all-start = ((bf16[8,3,2,16,1024]{4,3,2,1,0:T(8,128)(2,1)}), bf16[8,3,2,16,1024]{4,3,2,1,0:T(8,128)(2,1)}, u32[]{:S(2)}, u32[]{:S(2)}) async-start(bf16[8,3,2,16,1024]{4,3,2,1,0:T(8,128)(2,1)} %broadcast_select_fusion), calls=%async_computation | async-start | bytes 3145728 | tf_op jit(solution)/shard_map/all_to_all | solution.py:70
  22.2 74.2 %all-reduce.2.cloned.1.call-start = ((), (), s32[]{:S(2)}) async-start(), calls=%async_computation.2 | async-start | bytes 524288 | tf_op jit(solution)/shard_map/psum | solution.py:82
  23.1 36.6 %copy-start.2 = (bf16[16,2,1024]{2,1,0:T(2,128)(2,1)S(1)}, bf16[16,2,1024]{2,1,0:T(2,128)(2,1)}, u32[]{:S(2)}) copy-start(bf16[16,2,1024]{2,1,0:T(2,128)(2,1)} %param.15) | copy-start | bytes 196612
  59.8 4.5 %copy-start.1 = (bf16[16,3,2,16,1024]{4,3,2,1,0:T(8,128)(2,1)S(1)}, bf16[16,3,2,16,1024]{4,3,2,1,0:T(8,128)(2,1)}, u32[]{:S(2)}) copy-start(bf16[16,3,2,16,1024]{4,3,2,1,0:T(8,128)(2,1)} %gather_fusion.1) | copy-start | bytes 9437188
  70.4 5.4 %copy-start.7 = (f32[4096]{0:T(1024)S(1)}, f32[4096]{0:T(1024)}, u32[]{:S(2)}) copy-start(f32[4096]{0:T(1024)} %param.21) | copy-start | bytes 49156
  70.4 25.9 %copy-start.3 = (bf16[16,4096]{1,0:T(8,128)(2,1)S(1)}, bf16[16,4096]{1,0:T(8,128)(2,1)}, u32[]{:S(2)}) copy-start(bf16[16,4096]{1,0:T(8,128)(2,1)} %param.13) | copy-start | bytes 393220
  75.8 34.1 %reduce-scatter.2.cloned.1.call-start = ((), (), s32[]{:S(2)}) async-start(), calls=%async_computation.3 | async-start | bytes 98304 | tf_op jit(solution)/shard_map/reduce_scatter | solution.py:89
  97.5 3.6 %copy-start.8 = (s32[8,8]{1,0:T(8,128)S(1)}, s32[8,8]{1,0:T(8,128)}, u32[]{:S(2)}) copy-start(s32[8,8]{1,0:T(8,128)} %param.19) | copy-start | bytes 772
  97.5 13.3 %copy-start.6 = (f32[1024]{0:T(1024)S(1)}, f32[1024]{0:T(1024)}, u32[]{:S(2)}) copy-start(f32[1024]{0:T(1024)} %param.24) | copy-start | bytes 12292
Sparse Core Ops, SparseCore 0:
  75.9 20.4 all-reduce.1
  101.2 8.5 reduce-scatter.1
where the time goes:
time: 122 us; the launch traced here: 120 us
  waiting for transfers between devices  61.2 us (50%)
  matrix products  14.5 us (12%)
  between operations  14.3 us (12%)
  local copies, waits for them, and re-layouts  12.9 us (11%)
  other arithmetic  11.3 us (9%)
  starting transfers between devices  6.34 us (5%)
    all_to_all x1, waiting for transfers between devices, on_device(): lax.all_to_all(outbound, 'dp', split_axis=0, concat_axis=0, tiled=True)  32.8 us
    psum x1, waiting for transfers between devices, on_device(): summed = lax.psum(partial_out, 'mp')  20.5 us
    reduce_scatter x1, waiting for transfers between devices, on_device(): lax.psum_scatter(lifted, 'mp', scatter_dimension=0, tiled=True)  7.94 us
    all_to_all x1, starting transfers between devices, on_device(): lax.all_to_all(outbound, 'dp', split_axis=0, concat_axis=0, tiled=True)  6.3 us
    dot_general x1, matrix products, on_device(): jnp.dot(attention, out_weight, preferred_element_type=jnp.float32)  5.33 us
    select_n x2, other arithmetic, write_new(): jnp.where(landed[:, :, None, :, None], new_kv[:, None, :, None, :], kv_pa...  4.85 us
    gather x1, local copies, waits for them, and re-layouts, on_device(): outbound = kv_pool[slot_ids]  3.96 us
    gather x1, local copies, waits for them, and re-layouts, on_device(): fetched = inbound[holder]  3.82 us
  transfers between devices with their start and end apart: 3, of which 3 were waited for; matrix products, arithmetic and copies ran while one was open for 1% of the time, Pallas kernels for 0%

commit v1 on v0

v1 whole, which is shorter than its diff:
```python
import functools

import jax
import jax.numpy as jnp
from jax import lax
from jax.experimental import pallas as pl
from jax.experimental.pallas import tpu as pltpu
from jax.sharding import PartitionSpec as P

HD = 128
PAGES = 3
GROUP = 8
COLS = 512
EARLY = 7
F32 = jnp.float32
BF16 = jnp.bfloat16
MESH = pl.DeviceIdType.MESH


def iota(shape, dim):
    return lax.broadcasted_iota(jnp.int32, shape, dim)


def attend_group(pages_of, q8s, k8s, v8s, lens):
    heads = q8s[0].shape[0]
    width = heads * HD
    own = (iota((heads, width), 1) // HD) == iota((heads, width), 0)
    scores, heres = [], []
    for j in range(len(q8s)):
        keys = jnp.concatenate([pages_of(j, p, 0) for p in range(PAGES)], axis=0)
        place = iota((heads, keys.shape[0]), 1)
        spread = jnp.where(own, jnp.concatenate([q8s[j]] * heads, axis=1), 0.0).astype(BF16)
        s = lax.dot_general(spread, keys, (((1,), (1,)), ((), ())), preferred_element_type=F32)
        s = s * HD ** (-0.5)
        fresh = jnp.sum(q8s[j] * k8s[j], axis=1, keepdims=True) * HD ** (-0.5)
        here = place == lens[j]
        s = jnp.where(here, fresh, s)
        scores.append(jnp.where(place <= lens[j], s, -jnp.inf))
        heres.append(here)
    s = jnp.concatenate(scores, axis=0)
    e = jnp.exp(s - jnp.max(s, axis=1, keepdims=True))
    w = (e / jnp.sum(e, axis=1, keepdims=True)).astype(BF16).astype(F32)
    row = iota((heads, HD), 0)
    results = []
    for j in range(len(q8s)):
        mine = w[j * heads:(j + 1) * heads]
        values = jnp.concatenate([pages_of(j, p, 1) for p in range(PAGES)], axis=0)
        old = jnp.where(heres[j], 0.0, mine).astype(BF16)
        mixed = jnp.dot(old, values, preferred_element_type=F32)
        total = jnp.sum(jnp.where(heres[j], mine, 0.0), axis=1, keepdims=True) * v8s[j]
        for h in range(heads):
            total = total + jnp.where(row == h, mixed[:, h * HD:(h + 1) * HD], 0.0)
        results.append(total)
    return results


def main_kernel(n, rec, lens, rec_t, len_row, qkv, residual, tokens, norm_gain, depth_gain,
                pool, out_w, depth_in, code_embed, depth_head,
                inbound, logits,
                held, outbound, resident, ow_v, di_v, ce_v, dh_v,
                qkv3, msg32, msg, msg_in, rep, rep_in, local,
                po_send, po_mine, po_in, ss_send, ss_in, lf, lf_in, emb, base_s,
                held_sem, load_sem, msg_ss, msg_rs, page_ss, page_rs, rep_ss, rep_rs, mp_ss, mp_rs):
    g, me, m = lax.axis_index("groups"), lax.axis_index("dp"), lax.axis_index("mp")
    sessions = residual.shape[0]
    width = qkv.shape[1] // 3
    heads = width // HD
    homes = sessions * PAGES
    rows = rec_t.shape[1]
    half = residual.shape[1] // 2
    features = residual.shape[1]

    load_held = pltpu.make_async_copy(pool.at[pl.ds(homes, held.shape[0])], held, held_sem)
    load_held.start()

    def peer(shift):
        return (g, lax.rem(me + shift + n, n), m)

    partner = (g, me, 1 - m)
    barrier = pltpu.get_barrier_semaphore()
    for s in range(1, n):
        pl.semaphore_signal(barrier, inc=1, device_id=peer(s), device_id_type=MESH)
    pl.semaphore_signal(barrier, inc=1, device_id=partner, device_id_type=MESH)

    session, holder = rec_t[0:1, :], rec_t[1:2, :]
    behind = me - holder
    behind = jnp.where(behind < 0, behind + n, behind)
    is_session = jnp.where(session == iota((sessions, rows), 0) + me * sessions, 1.0, 0.0).astype(BF16)
    is_slot = jnp.where(behind == iota((n, rows), 0), 1.0, 0.0).astype(BF16)
    nt = (((1,), (1,)), ((), ()))
    pair = lax.dot_general(is_session, is_slot, nt, preferred_element_type=F32)
    pair_t = lax.dot_general(is_slot, is_session, nt, preferred_element_type=F32).astype(BF16)
    eye = iota((sessions, sessions), 0) == iota((sessions, sessions), 1)
    len_col = jnp.sum(jnp.where(eye, len_row[...].astype(F32), 0.0), axis=1, keepdims=True)
    len_wide = jnp.broadcast_to(len_col, (sessions, HD)).astype(BF16)
    sent = jnp.dot(pair_t, qkv[...], preferred_element_type=F32)
    sent_len = jnp.dot(pair_t, len_wide, preferred_element_type=F32)
    for c in range(3 * heads):
        msg32[:, c, :] = sent[:, c * HD:(c + 1) * HD]
    for c in range(heads):
        msg32[:, 3 * heads + c, :] = sent_len
    msg[...] = msg32[...].astype(BF16)

    def find(r, bases):
        ahead = rec[r, 2] - me
        ahead = jnp.where(ahead < 0, ahead + n, ahead)
        ahead = jnp.where(rec[r, 1] == me, ahead, -1)
        first = rec[r, 4] - homes
        return tuple(jnp.where(ahead == s, first, b) for s, b in enumerate(bases))

    bases = lax.fori_loop(0, rows, find, tuple(jnp.int32(0) for _ in range(n)))
    for s in range(n):
        base_s[s] = jnp.clip(bases[s], 0, held.shape[0] - PAGES)

    pl.semaphore_wait(barrier, n)
    msgs, pages, reps = [], [], []
    for s in range(1, n):
        c = pltpu.make_async_remote_copy(msg.at[s], msg_in.at[s], msg_ss.at[s], msg_rs.at[s],
                                         device_id=peer(-s), device_id_type=MESH)
        c.start()
        msgs.append(c)
        pages.append(pltpu.make_async_remote_copy(
            outbound.at[s], inbound.at[s], page_ss.at[s], page_rs.at[s],
            device_id=peer(s), device_id_type=MESH))
        reps.append(pltpu.make_async_remote_copy(
            rep.at[s], rep_in.at[s], rep_ss.at[s], rep_rs.at[s],
            device_id=peer(s), device_id_type=MESH))
    load_held.wait()
    for s in range(n):
        for p in range(PAGES):
            outbound[s, p] = held[base_s[s] + p]
        if 1 <= s <= EARLY:
            pages[s - 1].start()

    loads = [
        pltpu.make_async_copy(src, dst, load_sem.at[i])
        for i, (src, dst) in enumerate([
            (pool.at[pl.ds(0, homes)], resident), (out_w, ow_v), (depth_in, di_v),
            (code_embed, ce_v), (depth_head, dh_v)])
    ]
    for c in loads:
        c.start()

    wide = qkv[...].astype(F32)
    for c in range(3 * heads):
        qkv3[:, c, :] = wide[:, c * HD:(c + 1) * HD]
    msg_in[0] = jnp.zeros_like(msg_in[0])
    rep_in[0] = jnp.zeros_like(rep_in[0])

    for c in msgs:
        c.wait_recv()

    @pl.loop(0, n // GROUP)
    def _(t):
        at = [t * GROUP + j for j in range(GROUP)]
        got = [msg_in[a].astype(F32) for a in at]
        out = attend_group(
            lambda j, p, kv: outbound[at[j], p, kv],
            [x[0:heads] for x in got], [x[heads:2 * heads] for x in got],
            [x[2 * heads:3 * heads] for x in got],
            [x[3 * heads:4 * heads, 0:1].astype(jnp.int32) for x in got])
        for j in range(GROUP):
            rep[at[j]] = out[j]

    for c in reps:
        c.start()
    for s in range(EARLY + 1, n):
        pages[s - 1].start()

    loads[0].wait()

    @pl.loop(0, sessions // GROUP)
    def _(t):
        at = [t * GROUP + j for j in range(GROUP)]
        got = [qkv3[a] for a in at]
        out = attend_group(
            lambda j, p, kv: resident[at[j] * PAGES + p, kv],
            [x[0:heads] for x in got], [x[heads:2 * heads] for x in got],
            [x[2 * heads:3 * heads] for x in got], [lens[a] for a in at])
        for j in range(GROUP):
            local[at[j]] = out[j]

    loads[3].wait()
    count, books = tokens.shape
    entries = code_embed.shape[0]
    diag = iota((books, books), 0) == iota((books, books), 1)
    picks = []
    for b in range(count):
        col = jnp.sum(jnp.where(diag, tokens[b:b + 1, :].astype(F32), 0.0), axis=1, keepdims=True)
        hit = col.astype(jnp.int32) == iota((books, entries), 1)
        picks.append(jnp.where(hit, 1.0, 0.0))
    pick = jnp.concatenate(picks, axis=0).astype(BF16)

    @pl.loop(0, emb.shape[1] // COLS)
    def _(t):
        at = pl.ds(pl.multiple_of(t * COLS, COLS), COLS)
        emb[:, at] = jnp.dot(pick, ce_v[:, at], preferred_element_type=F32)

    for c in reps:
        c.wait_recv()
    here = jnp.concatenate([local[:, h, :] for h in range(heads)], axis=1)
    away = jnp.concatenate([rep_in[:, h, :] for h in range(heads)], axis=1).astype(BF16)
    away = jnp.dot(pair.astype(BF16), away, preferred_element_type=F32)
    linked = jnp.sum(pair, axis=1, keepdims=True) > 0.0
    attention = jnp.where(linked, away, here).astype(BF16)

    loads[1].wait()

    def project(first, target):
        @pl.loop(0, half // COLS)
        def _(t):
            at = pl.ds(pl.multiple_of(first + t * COLS, COLS), COLS)
            to = pl.ds(pl.multiple_of(t * COLS, COLS), COLS)
            target[:, to] = jnp.dot(attention, ow_v[:, at], preferred_element_type=F32)

    def swap(i, src, dst):
        c = pltpu.make_async_remote_copy(src, dst, mp_ss.at[i], mp_rs.at[i],
                                         device_id=partner, device_id_type=MESH)
        c.start()
        return c

    project((1 - m) * half, po_send)
    swap0 = swap(0, po_send, po_in)
    project(m * half, po_mine)
    swap0.wait_recv()
    my_half = pl.ds(pl.multiple_of(m * half, half), half)
    layer = residual[:, my_half].astype(F32) + (po_mine[...] + po_in[...])
    layer = layer.astype(BF16).astype(F32)
    squares = jnp.sum(layer * layer, axis=1, keepdims=True)
    ss_send[...] = jnp.broadcast_to(squares, ss_send.shape)
    swap1 = swap(1, ss_send, ss_in)
    loads[2].wait()
    swap1.wait_recv()
    squares = squares + ss_in[:, 0:1]
    normed = (layer * lax.rsqrt(squares * (1.0 / features) + 1e-05) * norm_gain[:, my_half]).astype(BF16)
    for t in range(lf.shape[1] // COLS):
        at = slice(t * COLS, (t + 1) * COLS)
        lf[:, at] = jnp.dot(normed, di_v[:, at], preferred_element_type=F32)
    swap2 = swap(2, lf.at[pl.ds(pl.multiple_of((1 - m) * count, count), count)], lf_in)
    loads[4].wait()
    swap2.wait_recv()
    lifted = lf[pl.ds(pl.multiple_of(m * count, count), count), :] + lf_in[...]
    parts = []
    for b in range(count):
        hidden = lifted[b:b + 1, :] + emb[b * books:(b + 1) * books, :]
        mean = jnp.mean(hidden * hidden, axis=1, keepdims=True)
        parts.append(hidden * lax.rsqrt(mean + 1e-05) * depth_gain[...])
    depth_normed = jnp.concatenate(parts, axis=0).astype(BF16)
    for t in range(logits.shape[1] // COLS):
        at = slice(t * COLS, (t + 1) * COLS)
        logits[:, at] = jnp.dot(depth_normed, dh_v[:, at], preferred_element_type=F32).astype(BF16)

    for c in (swap0, swap1, swap2):
        c.wait_send()
    for c in msgs + reps:
        c.wait_send()
    for c in pages:
        c.wait_send()
    for c in pages:
        c.wait_recv()


def place_kernel(n, rec, lens, qkv, pool, inbound, logits_in, cache, logits, buf, slot, pages,
                 in_sem, out_sem, log_sem):
    me = lax.axis_index("dp")
    sessions = qkv.shape[0]
    width = qkv.shape[1] // 3
    copy_logits = pltpu.make_async_copy(logits_in, logits, log_sem)
    copy_logits.start()
    for i in range(sessions):
        slot[i] = 0

    @pl.loop(0, rec.shape[0])
    def _(r):
        @pl.when(rec[r, 2] == me)
        def _():
            behind = me - rec[r, 1]
            i = rec[r, 0] - me * sessions
            slot[i] = jnp.where(behind < 0, behind + n, behind)
            pages[i] = rec[r, 3]

    def space(i):
        return buf.at[pl.ds(i * PAGES, PAGES)]

    @pl.loop(0, sessions)
    def _(i):
        @pl.when(slot[i] == 0)
        def _():
            pltpu.make_async_copy(pool.at[pl.ds(i * PAGES, PAGES)], space(i), in_sem.at[i]).start()

        @pl.when(slot[i] != 0)
        def _():
            pltpu.make_async_copy(inbound.at[slot[i]], space(i), in_sem.at[i]).start()

    def give(i):
        return pltpu.make_async_copy(space(i), cache.at[pl.ds(i * PAGES, PAGES)], out_sem.at[i])

    for i in range(sessions):
        pltpu.make_async_copy(pool.at[pl.ds(i * PAGES, PAGES)], space(i), in_sem.at[i]).wait()

        @pl.when(slot[i] != 0)
        def _():
            for p in range(PAGES):
                @pl.when(p >= pages[i])
                def _():
                    buf[i * PAGES + p] = jnp.zeros(buf.shape[1:], BF16)

        size = buf.shape[2]
        page = i * PAGES + lens[i] // size
        hit = iota((size, width), 0) == lax.rem(lens[i], size)
        for kv in range(2):
            new = qkv[:, (1 + kv) * width:(2 + kv) * width].astype(F32)[i:i + 1, :]
            buf[page, kv] = jnp.where(hit, new, buf[page, kv].astype(F32)).astype(BF16)
        give(i).start()
    for i in range(sessions):
        give(i).wait()
    copy_logits.wait()


def on_device(n, residual, queries, new_kv, kv_pool, cache_len, reconnect, audio_tokens, out_weight,
              norm_gain, depth_in, code_embed, depth_gain, depth_head):
    sessions, width = queries.shape
    heads = width // HD
    qkv = jnp.concatenate([queries, new_kv.reshape(sessions, 2 * width)], axis=1)
    count, books = audio_tokens.shape
    page = kv_pool.shape[1:]
    homes = sessions * PAGES
    features = residual.shape[1]
    half = features // 2
    depth = depth_in.shape[1]
    entries = depth_head.shape[1]
    vmem = pl.BlockSpec(memory_space=pltpu.VMEM)
    smem = pl.BlockSpec(memory_space=pltpu.SMEM)
    anywhere = pl.BlockSpec(memory_space=pl.ANY)
    dma = pltpu.SemaphoreType.DMA
    inbound, logits = pl.pallas_call(
        functools.partial(main_kernel, n),
        out_shape=(jax.ShapeDtypeStruct((n, PAGES) + page, BF16),
                   jax.ShapeDtypeStruct((count * books, entries), BF16)),
        in_specs=[smem, smem] + [vmem] * 7 + [anywhere] * 5,
        out_specs=(anywhere, vmem),
        scratch_shapes=[
            pltpu.VMEM((kv_pool.shape[0] - homes,) + page, BF16),
            pltpu.VMEM((n, PAGES) + page, BF16),
            pltpu.VMEM((homes,) + page, BF16),
            pltpu.VMEM(out_weight.shape, BF16),
            pltpu.VMEM(depth_in.shape, BF16),
            pltpu.VMEM(code_embed.shape, BF16),
            pltpu.VMEM(depth_head.shape, BF16),
            pltpu.VMEM((sessions, 3 * heads, HD), F32),
            pltpu.VMEM((n, 4 * heads, HD), F32),
            pltpu.VMEM((n, 4 * heads, HD), BF16),
            pltpu.VMEM((n, 4 * heads, HD), BF16),
            pltpu.VMEM((n, heads, HD), F32),
            pltpu.VMEM((n, heads, HD), F32),
            pltpu.VMEM((sessions, heads, HD), F32),
            pltpu.VMEM((sessions, half), F32),
            pltpu.VMEM((sessions, half), F32),
            pltpu.VMEM((sessions, half), F32),
            pltpu.VMEM((sessions, HD), F32),
            pltpu.VMEM((sessions, HD), F32),
            pltpu.VMEM((sessions, depth), F32),
            pltpu.VMEM((count, depth), F32),
            pltpu.VMEM((count * books, depth), F32),
            pltpu.SMEM((n,), jnp.int32),
            dma, dma((5,)), dma((n,)), dma((n,)), dma((n,)), dma((n,)), dma((n,)), dma((n,)),
            dma((3,)), dma((3,)),
        ],
        compiler_params=pltpu.CompilerParams(
            collective_id=0, has_side_effects=True, vmem_limit_bytes=48 * 1024 * 1024),
        name="serve",
    )(reconnect, cache_len, reconnect.T, cache_len.reshape(1, sessions), qkv, residual, audio_tokens,
      norm_gain.reshape(1, features), depth_gain.reshape(1, depth),
      kv_pool, out_weight, depth_in, code_embed, depth_head)
    new_cache, logits = pl.pallas_call(
        functools.partial(place_kernel, n),
        out_shape=(jax.ShapeDtypeStruct((homes,) + page, BF16),
                   jax.ShapeDtypeStruct((count * books, entries), BF16)),
        in_specs=[smem, smem, vmem, anywhere, anywhere, anywhere],
        out_specs=(anywhere, anywhere),
        scratch_shapes=[
            pltpu.VMEM((homes,) + page, BF16),
            pltpu.SMEM((sessions,), jnp.int32),
            pltpu.SMEM((sessions,), jnp.int32),
            dma((sessions,)), dma((sessions,)), dma,
        ],
        compiler_params=pltpu.CompilerParams(vmem_limit_bytes=32 * 1024 * 1024),
        name="place",
    )(reconnect, cache_len, qkv, kv_pool, inbound, logits)
    return (logits.reshape(count, books, entries), new_cache)


def solution(mesh):
    in_specs = (
        P(("groups", "dp"), None),
        P(("groups", "dp"), "mp"),
        P(("groups", "dp"), None, "mp"),
        P(("groups", "dp"), None, None, "mp"),
        P(("groups", "dp")),
        P("groups", None),
        P(("groups", "dp", "mp"), None),
        P("mp", None),
        P(),
        P("mp", None),
        P(),
        P(),
        P(),
    )
    out_specs = (P(("groups", "dp", "mp"), None, None), P(("groups", "dp"), None, None, "mp"))
    return jax.shard_map(
        functools.partial(on_device, mesh.shape["dp"]), mesh=mesh, in_specs=in_specs,
        out_specs=out_specs, check_vma=False
    )
```

time: 122 us -> 68.2 us (0.56)
  the two profiles are of different devices: /device:TPU:18 before, /device:TPU:0 now
where the time goes in v1:
time: 68.2 us; the launch traced here: 67.7 us
  Pallas kernels  57.1 us (84%)
  local copies, waits for them, and re-layouts  9.9 us (15%)
    pallas_call x1, Pallas kernels, on_device(): pl.pallas_call(functools.partial(main_kernel, n), out_shape=(jax.ShapeDty...  49.6 us
    unnamed x21, local copies, waits for them, and re-layouts  9.9 us
    pallas_call x1, Pallas kernels, on_device(): pl.pallas_call(functools.partial(place_kernel, n), out_shape=(jax.ShapeDt...  7.59 us

profile of v1, /device:TPU:0, one launch (start us, length us, event | category | flops | bytes accessed | tf_op | source)
XLA Modules:
  0.0 67.7 jit_solution(15129704463812013680)
XLA Ops:
  0.6 0.8 %copy.16.rec = s32[32,5]{1,0:T(8,128)S(1)} copy(s32[32,5]{0,1:T(8,128)} %param.18) | data formatting | bytes 1280 | tf_op args[5]
  1.4 0.9 %copy.17 = bf16[2,8,2,1024]{3,1,2,0:T(8,128)(2,1)S(1)} copy(bf16[2,8,2,1024]{3,2,1,0:T(2,128)(2,1)} %bitcast.12) | data formatting | bytes 131072
  2.3 0.8 %constant_dynamic-update-slice_fusion.1 = bf16[16,3072]{1,0:T(8,128)(2,1)S(1)} fusion(bf16[16,1024]{1,0:T(8,128)(2,1)} %param.14), kind=kLoop, calls=%fused_computation.1 | loop fusion | bytes 65536
  3.0 0.0 copy-start.1
  3.0 1.6 %copy-done.1 = bf16[1024,1024]{1,0:T(8,128)(2,1)S(1)} copy-done((bf16[1024,1024]{1,0:T(8,128)(2,1)S(1)}, bf16[1024,1024]{1,0:T(8,128)(2,1)}, u32[]{:S(2)}) %copy-start.1) | copy-done | bytes 2097176
  4.6 0.0 copy-start.2
  4.6 1.6 %copy-done.2 = bf16[1024,1024]{1,0:T(8,128)(2,1)S(1)} copy-done((bf16[1024,1024]{1,0:T(8,128)(2,1)S(1)}, bf16[1024,1024]{1,0:T(8,128)(2,1)}, u32[]{:S(2)}) %copy-start.2) | copy-done | bytes 2097176
  6.2 0.0 copy-start.3
  6.2 0.9 %copy-done.3 = bf16[16,4096]{1,0:T(8,128)(2,1)S(1)} copy-done((bf16[16,4096]{1,0:T(8,128)(2,1)S(1)}, bf16[16,4096]{1,0:T(8,128)(2,1)}, u32[]{:S(2)}) %copy-start.3) | copy-done | bytes 131096
  7.1 0.0 copy-start.4
  7.1 0.7 %copy-done.4 = f32[4096]{0:T(1024)S(1)} copy-done((f32[4096]{0:T(1024)S(1)}, f32[4096]{0:T(1024)}, u32[]{:S(2)}) %copy-start.4) | copy-done | bytes 16408
  7.8 0.0 copy-start.5
  7.8 0.7 %copy-done.5 = s32[32,5]{0,1:T(8,128)S(1)} copy-done((s32[32,5]{0,1:T(8,128)S(1)}, s32[32,5]{0,1:T(8,128)}, u32[]{:S(2)}) %copy-start.5) | copy-done | bytes 664
  8.5 0.0 copy-start.6
  8.5 0.7 copy-done.6
  9.2 0.0 copy-start.7
  9.2 0.7 %copy-done.7 = s32[8,8]{1,0:T(8,128)S(1)} copy-done((s32[8,8]{1,0:T(8,128)S(1)}, s32[8,8]{1,0:T(8,128)}, u32[]{:S(2)}) %copy-start.7) | copy-done | bytes 280
  9.9 0.0 copy-start.8
  9.9 0.7 %copy-done.8 = f32[1024]{0:T(1024)S(1)} copy-done((f32[1024]{0:T(1024)S(1)}, f32[1024]{0:T(1024)}, u32[]{:S(2)}) %copy-start.8) | copy-done | bytes 4120
  10.5 0.0 copy-start
  10.6 49.6 %serve.1 = (bf16[8,3,2,16,1024]{4,3,2,1,0:T(8,128)(2,1)S(1)}, bf16[64,1024]{1,0:T(8,128)(2,1)S(1)}) custom-call(s32[32,5]{1,0:T(8,128)S(1)} %copy.16.rec, s32[16]{0:T(128)S(1)} %copy-done.6, s32[5,32]{1,0:T(8,128)S(1)} %bitcast.8, s32[1,16]{1,0:T(1,128)S(1)} %bitcast.9, bf16[16,3072]{1,0:T(8,128)(2,1)S(1)} %constant_dynamic-update-slice_fusion.qkv, ...), custom_call_target="tpu_custom_call" | custom-call | tf_op jit(solution)/shard_map/serve/pallas_call | solution.py:336
  60.1 0.0 copy-done
  60.1 7.6 %place.1 = (bf16[48,2,16,1024]{3,2,1,0:T(8,128)(2,1)}, bf16[64,1024]{1,0:T(8,128)(2,1)}) custom-call(s32[32,5]{1,0:T(8,128)S(1)} %copy.16.rec, s32[16]{0:T(128)S(1)} %copy-done.6, bf16[16,3072]{1,0:T(8,128)(2,1)S(1)} %constant_dynamic-update-slice_fusion.qkv, bf16[60,2,16,1024]{3,2,1,0:T(8,128)(2,1)S(1)} %copy-done, ...), custom_call_target="tpu_custom_call" | custom-call | tf_op jit(solution)/shard_map/place/pallas_call | solution.py:375
  (1 shorter events, 0.0 us)
Async XLA Ops:
  3.0 1.6 %copy-start.1 = (bf16[1024,1024]{1,0:T(8,128)(2,1)S(1)}, bf16[1024,1024]{1,0:T(8,128)(2,1)}, u32[]{:S(2)}) copy-start(bf16[1024,1024]{1,0:T(8,128)(2,1)} %code_embed.1) | copy-start | bytes 6291460
  4.6 1.6 %copy-start.2 = (bf16[1024,1024]{1,0:T(8,128)(2,1)S(1)}, bf16[1024,1024]{1,0:T(8,128)(2,1)}, u32[]{:S(2)}) copy-start(bf16[1024,1024]{1,0:T(8,128)(2,1)} %depth_head.1) | copy-start | bytes 6291460
  6.2 0.9 %copy-start.3 = (bf16[16,4096]{1,0:T(8,128)(2,1)S(1)}, bf16[16,4096]{1,0:T(8,128)(2,1)}, u32[]{:S(2)}) copy-start(bf16[16,4096]{1,0:T(8,128)(2,1)} %residual.1) | copy-start | bytes 393220
  7.1 0.7 %copy-start.4 = (f32[4096]{0:T(1024)S(1)}, f32[4096]{0:T(1024)}, u32[]{:S(2)}) copy-start(f32[4096]{0:T(1024)} %param.21) | copy-start | bytes 49156
  7.8 0.7 %copy-start.5 = (s32[32,5]{0,1:T(8,128)S(1)}, s32[32,5]{0,1:T(8,128)}, u32[]{:S(2)}) copy-start(s32[32,5]{0,1:T(8,128)} %param.18) | copy-start | bytes 1924
  8.5 0.7 copy-start.6
  9.2 0.7 %copy-start.7 = (s32[8,8]{1,0:T(8,128)S(1)}, s32[8,8]{1,0:T(8,128)}, u32[]{:S(2)}) copy-start(s32[8,8]{1,0:T(8,128)} %tokens.1) | copy-start | bytes 772
  9.9 0.7 %copy-start.8 = (f32[1024]{0:T(1024)S(1)}, f32[1024]{0:T(1024)}, u32[]{:S(2)}) copy-start(f32[1024]{0:T(1024)} %param.24) | copy-start | bytes 12292
  10.5 49.6 %copy-start = (bf16[60,2,16,1024]{3,2,1,0:T(8,128)(2,1)S(1)}, bf16[60,2,16,1024]{3,2,1,0:T(8,128)(2,1)}, u32[]{:S(2)}) copy-start(bf16[60,2,16,1024]{3,2,1,0:T(8,128)(2,1)} %pool.3) | copy-start | bytes 11796484

commit v2 on v1

--- a/solution.py
+++ b/solution.py
@@ -11,7 +11,7 @@
 PAGES = 3
 GROUP = 8
 COLS = 512
-EARLY = 7
+EARLY = 2
 F32 = jnp.float32
 BF16 = jnp.bfloat16
 MESH = pl.DeviceIdType.MESH
@@ -54,16 +54,35 @@
     return results
 
 
-def main_kernel(n, rec, lens, rec_t, len_row, qkv, residual, tokens, norm_gain, depth_gain,
+def settle(cache, pages, h, length, new, count):
+    size, width = cache.shape[2:]
+    for p, at in enumerate(pages):
+        old = cache[at, h].astype(F32)
+        if count is not None:
+            old = jnp.where(p < count, old, 0.0)
+        hit = iota((size, width), 0) + p * size == length
+        cache[at, h] = jnp.where(hit, new, old).astype(BF16)
+
+
+def main_kernel(n, rec, lens, *refs):
+    small_in, (pool, out_w, depth_in, code_embed, depth_head), (inbound, resident, logits) = (
+        refs[:8], refs[8:13], refs[13:16])
+    rec_t, len_row, queries, kv, residual, tokens, norm_gain, depth_gain = small = refs[16:24]
+    run_main(n, rec, lens, rec_t, len_row, queries, kv, residual, tokens, norm_gain, depth_gain,
+             pool, out_w, depth_in, code_embed, depth_head, inbound, resident, logits,
+             small_in, small, *refs[24:])
+
+
+def run_main(n, rec, lens, rec_t, len_row, queries, kv, residual, tokens, norm_gain, depth_gain,
                 pool, out_w, depth_in, code_embed, depth_head,
-                inbound, logits,
-                held, outbound, resident, ow_v, di_v, ce_v, dh_v,
+                inbound, resident, logits, small_in, small,
+                held, outbound, ow_v, di_v, ce_v, dh_v, kv32, sent_kv, sent_len_v, small_sem,
                 qkv3, msg32, msg, msg_in, rep, rep_in, local,
                 po_send, po_mine, po_in, ss_send, ss_in, lf, lf_in, emb, base_s,
                 held_sem, load_sem, msg_ss, msg_rs, page_ss, page_rs, rep_ss, rep_rs, mp_ss, mp_rs):
     g, me, m = lax.axis_index("groups"), lax.axis_index("dp"), lax.axis_index("mp")
     sessions = residual.shape[0]
-    width = qkv.shape[1] // 3
+    width = queries.shape[1]
     heads = width // HD
     homes = sessions * PAGES
     rows = rec_t.shape[1]
@@ -72,6 +91,10 @@
 
     load_held = pltpu.make_async_copy(pool.at[pl.ds(homes, held.shape[0])], held, held_sem)
     load_held.start()
+    fetch = [pltpu.make_async_copy(src, dst, small_sem.at[i])
+             for i, (src, dst) in enumerate(zip(small_in, small))]
+    for c in fetch:
+        c.start()
 
     def peer(shift):
         return (g, lax.rem(me + shift + n, n), m)
@@ -81,6 +104,10 @@
     for s in range(1, n):
         pl.semaphore_signal(barrier, inc=1, device_id=peer(s), device_id_type=MESH)
     pl.semaphore_signal(barrier, inc=1, device_id=partner, device_id_type=MESH)
+
+    for c in fetch:
+        c.wait()
+    kv32[...] = kv[...].astype(F32)
 
     session, holder = rec_t[0:1, :], rec_t[1:2, :]
     behind = me - holder
@@ -93,8 +120,11 @@
     eye = iota((sessions, sessions), 0) == iota((sessions, sessions), 1)
     len_col = jnp.sum(jnp.where(eye, len_row[...].astype(F32), 0.0), axis=1, keepdims=True)
     len_wide = jnp.broadcast_to(len_col, (sessions, HD)).astype(BF16)
-    sent = jnp.dot(pair_t, qkv[...], preferred_element_type=F32)
-    sent_len = jnp.dot(pair_t, len_wide, preferred_element_type=F32)
+    sent = jnp.concatenate(
+        [jnp.dot(pair_t, x, preferred_element_type=F32)
+         for x in (queries[...], kv32[:, 0, :].astype(BF16), kv32[:, 1, :].astype(BF16))], axis=1)
+    sent_kv[...] = sent[:, width:]
+    sent_len_v[...] = sent_len = jnp.dot(pair_t, len_wide, preferred_element_type=F32)
     for c in range(3 * heads):
         msg32[:, c, :] = sent[:, c * HD:(c + 1) * HD]
     for c in range(heads):
@@ -102,10 +132,10 @@
     msg[...] = msg32[...].astype(BF16)
 
     def find(r, bases):
-        ahead = rec[r, 2] - me
+        ahead = rec[2, r] - me
         ahead = jnp.where(ahead < 0, ahead + n, ahead)
-        ahead = jnp.where(rec[r, 1] == me, ahead, -1)
-        first = rec[r, 4] - homes
+        ahead = jnp.where(rec[1, r] == me, ahead, -1)
+        first = rec[4, r] - homes
         return tuple(jnp.where(ahead == s, first, b) for s, b in enumerate(bases))
 
     bases = lax.fori_loop(0, rows, find, tuple(jnp.int32(0) for _ in range(n)))
@@ -120,16 +150,17 @@
         c.start()
         msgs.append(c)
         pages.append(pltpu.make_async_remote_copy(
-            outbound.at[s], inbound.at[s], page_ss.at[s], page_rs.at[s],
+            outbound.at[s], inbound.at[pl.ds(s * PAGES, PAGES)], page_ss.at[s], page_rs.at[s],
             device_id=peer(s), device_id_type=MESH))
         reps.append(pltpu.make_async_remote_copy(
             rep.at[s], rep_in.at[s], rep_ss.at[s], rep_rs.at[s],
             device_id=peer(s), device_id_type=MESH))
     load_held.wait()
-    for s in range(n):
+    order = sorted(range(1, n), key=lambda s: abs(2 * s - n))
+    for k, s in enumerate(order + [0]):
         for p in range(PAGES):
             outbound[s, p] = held[base_s[s] + p]
-        if 1 <= s <= EARLY:
+        if k < EARLY:
             pages[s - 1].start()
 
     loads = [
@@ -141,7 +172,7 @@
     for c in loads:
         c.start()
 
-    wide = qkv[...].astype(F32)
+    wide = jnp.concatenate([queries[...].astype(F32), kv32[:, 0, :], kv32[:, 1, :]], axis=1)
     for c in range(3 * heads):
         qkv3[:, c, :] = wide[:, c * HD:(c + 1) * HD]
     msg_in[0] = jnp.zeros_like(msg_in[0])
@@ -164,7 +195,7 @@
 
     for c in reps:
         c.start()
-    for s in range(EARLY + 1, n):
+    for s in order[EARLY:]:
         pages[s - 1].start()
 
     loads[0].wait()
@@ -179,6 +210,11 @@
             [x[2 * heads:3 * heads] for x in got], [lens[a] for a in at])
         for j in range(GROUP):
             local[at[j]] = out[j]
+
+    for i in range(sessions):
+        for h in range(2):
+            settle(resident, (i * PAGES, i * PAGES + 1, i * PAGES + 2), h,
+                   lens[i], kv32[i, h:h + 1, :], None)
 
     loads[3].wait()
     count, books = tokens.shape
@@ -256,64 +292,42 @@
         c.wait_send()
     for c in pages:
         c.wait_send()
-    for c in pages:
-        c.wait_recv()
-
-
-def place_kernel(n, rec, lens, qkv, pool, inbound, logits_in, cache, logits, buf, slot, pages,
-                 in_sem, out_sem, log_sem):
+    mine = jnp.where(rec_t[2:3, :] == me, rec_t[3:4, :], 0)
+    total = jnp.sum(jnp.where(behind == iota((n, rows), 0), mine, 0).astype(F32), axis=1, keepdims=True)
+    for s in order:
+        pages[s - 1].wait_recv()
+        for h in range(2):
+            settle(inbound, tuple(s * PAGES + p for p in range(PAGES)), h,
+                   sent_len_v[s:s + 1, 0:1].astype(jnp.int32),
+                   sent_kv[s:s + 1, h * width:(h + 1) * width], total[s:s + 1].astype(jnp.int32))
+
+
+def place_kernel(n, rec, resident, inbound, logits_in, cache, logits, sem, log_sem):
     me = lax.axis_index("dp")
-    sessions = qkv.shape[0]
-    width = qkv.shape[1] // 3
+    sessions = resident.shape[0] // PAGES
     copy_logits = pltpu.make_async_copy(logits_in, logits, log_sem)
     copy_logits.start()
+
+    def from_holder(r, linked):
+        mine = rec[2, r] == me
+        i = rec[0, r] - me * sessions
+
+        @pl.when(mine)
+        def _():
+            behind = me - rec[1, r]
+            behind = jnp.where(behind < 0, behind + n, behind)
+            pltpu.make_async_copy(inbound.at[pl.ds(behind * PAGES, PAGES)],
+                                  cache.at[pl.ds(i * PAGES, PAGES)], sem).start()
+
+        return tuple(jnp.where(mine & (i == j), 1, x) for j, x in enumerate(linked))
+
+    linked = lax.fori_loop(0, rec.shape[1], from_holder, tuple(jnp.int32(0) for _ in range(sessions)))
     for i in range(sessions):
-        slot[i] = 0
-
-    @pl.loop(0, rec.shape[0])
-    def _(r):
-        @pl.when(rec[r, 2] == me)
+        @pl.when(linked[i] == 0)
         def _():
-            behind = me - rec[r, 1]
-            i = rec[r, 0] - me * sessions
-            slot[i] = jnp.where(behind < 0, behind + n, behind)
-            pages[i] = rec[r, 3]
-
-    def space(i):
-        return buf.at[pl.ds(i * PAGES, PAGES)]
-
-    @pl.loop(0, sessions)
-    def _(i):
-        @pl.when(slot[i] == 0)
-        def _():
-            pltpu.make_async_copy(pool.at[pl.ds(i * PAGES, PAGES)], space(i), in_sem.at[i]).start()
-
-        @pl.when(slot[i] != 0)
-        def _():
-            pltpu.make_async_copy(inbound.at[slot[i]], space(i), in_sem.at[i]).start()
-
-    def give(i):
-        return pltpu.make_async_copy(space(i), cache.at[pl.ds(i * PAGES, PAGES)], out_sem.at[i])
-
-    for i in range(sessions):
-        pltpu.make_async_copy(pool.at[pl.ds(i * PAGES, PAGES)], space(i), in_sem.at[i]).wait()
-
-        @pl.when(slot[i] != 0)
-        def _():
-            for p in range(PAGES):
-                @pl.when(p >= pages[i])
-                def _():
-                    buf[i * PAGES + p] = jnp.zeros(buf.shape[1:], BF16)
-
-        size = buf.shape[2]
-        page = i * PAGES + lens[i] // size
-        hit = iota((size, width), 0) == lax.rem(lens[i], size)
-        for kv in range(2):
-            new = qkv[:, (1 + kv) * width:(2 + kv) * width].astype(F32)[i:i + 1, :]
-            buf[page, kv] = jnp.where(hit, new, buf[page, kv].astype(F32)).astype(BF16)
-        give(i).start()
-    for i in range(sessions):
-        give(i).wait()
+            pltpu.make_async_copy(resident.at[pl.ds(i * PAGES, PAGES)],
+                                  cache.at[pl.ds(i * PAGES, PAGES)], sem).start()
+    pltpu.make_async_copy(resident, cache, sem).wait()
     copy_logits.wait()
 
 
@@ -321,7 +335,6 @@
               norm_gain, depth_in, code_embed, depth_gain, depth_head):
     sessions, width = queries.shape
     heads = width // HD
-    qkv = jnp.concatenate([queries, new_kv.reshape(sessions, 2 * width)], axis=1)
     count, books = audio_tokens.shape
     page = kv_pool.shape[1:]
     homes = sessions * PAGES
@@ -331,22 +344,34 @@
     entries = depth_head.shape[1]
     vmem = pl.BlockSpec(memory_space=pltpu.VMEM)
     smem = pl.BlockSpec(memory_space=pltpu.SMEM)
-    anywhere = pl.BlockSpec(memory_space=pl.ANY)
+    anywhere = pl.BlockSpec(memory_space=pltpu.HBM)
     dma = pltpu.SemaphoreType.DMA
-    inbound, logits = pl.pallas_call(
+    rec_t = reconnect.T
+    inputs = (rec_t, cache_len.reshape(1, sessions), queries, new_kv, residual, audio_tokens,
+              norm_gain.reshape(1, features), depth_gain.reshape(1, depth))
+    def stay(x):
+        return pltpu.with_memory_space_constraint(x, pltpu.HBM)
+
+    inputs = tuple(stay(x) for x in inputs)
+    large = tuple(stay(x) for x in (kv_pool, out_weight, depth_in, code_embed, depth_head))
+    inbound, resident, logits = pl.pallas_call(
         functools.partial(main_kernel, n),
-        out_shape=(jax.ShapeDtypeStruct((n, PAGES) + page, BF16),
+        out_shape=(jax.ShapeDtypeStruct((n * PAGES,) + page, BF16),
+                   jax.ShapeDtypeStruct((homes,) + page, BF16),
                    jax.ShapeDtypeStruct((count * books, entries), BF16)),
-        in_specs=[smem, smem] + [vmem] * 7 + [anywhere] * 5,
-        out_specs=(anywhere, vmem),
-        scratch_shapes=[
+        in_specs=[smem, smem] + [anywhere] * 13,
+        out_specs=(vmem, vmem, vmem),
+        scratch_shapes=[pltpu.VMEM(x.shape, x.dtype) for x in inputs] + [
             pltpu.VMEM((kv_pool.shape[0] - homes,) + page, BF16),
             pltpu.VMEM((n, PAGES) + page, BF16),
-            pltpu.VMEM((homes,) + page, BF16),
             pltpu.VMEM(out_weight.shape, BF16),
             pltpu.VMEM(depth_in.shape, BF16),
             pltpu.VMEM(code_embed.shape, BF16),
             pltpu.VMEM(depth_head.shape, BF16),
+            pltpu.VMEM(new_kv.shape, F32),
+            pltpu.VMEM((n, 2 * width), F32),
+            pltpu.VMEM((n, HD), F32),
+            dma((len(inputs),)),
             pltpu.VMEM((sessions, 3 * heads, HD), F32),
             pltpu.VMEM((n, 4 * heads, HD), F32),
             pltpu.VMEM((n, 4 * heads, HD), BF16),
@@ -367,26 +392,19 @@
             dma((3,)), dma((3,)),
         ],
         compiler_params=pltpu.CompilerParams(
-            collective_id=0, has_side_effects=True, vmem_limit_bytes=48 * 1024 * 1024),
+            collective_id=0, has_side_effects=True, vmem_limit_bytes=32 * 1024 * 1024),
         name="serve",
-    )(reconnect, cache_len, reconnect.T, cache_len.reshape(1, sessions), qkv, residual, audio_tokens,
-      norm_gain.reshape(1, features), depth_gain.reshape(1, depth),
-      kv_pool, out_weight, depth_in, code_embed, depth_head)
+    )(rec_t, cache_len, *inputs, *large)
     new_cache, logits = pl.pallas_call(
         functools.partial(place_kernel, n),
         out_shape=(jax.ShapeDtypeStruct((homes,) + page, BF16),
                    jax.ShapeDtypeStruct((count * books, entries), BF16)),
-        in_specs=[smem, smem, vmem, anywhere, anywhere, anywhere],
+        in_specs=[smem, vmem, vmem, vmem],
         out_specs=(anywhere, anywhere),
-        scratch_shapes=[
-            pltpu.VMEM((homes,) + page, BF16),
-            pltpu.SMEM((sessions,), jnp.int32),
-            pltpu.SMEM((sessions,), jnp.int32),
-            dma((sessions,)), dma((sessions,)), dma,
-        ],
-        compiler_params=pltpu.CompilerParams(vmem_limit_bytes=32 * 1024 * 1024),
+        scratch_shapes=[dma, dma],
+        compiler_params=pltpu.CompilerParams(vmem_limit_bytes=16 * 1024 * 1024),
         name="place",
-    )(reconnect, cache_len, qkv, kv_pool, inbound, logits)
+    )(rec_t, resident, inbound, logits)
     return (logits.reshape(count, books, entries), new_cache)
 
 

time: 68.2 us -> 46.3 us (0.68)
  the two profiles are of different devices: /device:TPU:0 before, /device:TPU:18 now
where the time goes in v2:
time: 46.3 us; the launch traced here: 46.1 us
  Pallas kernels  45.4 us (98%)
  between operations  0.66 us (1%)
    pallas_call x1, Pallas kernels, on_device(): pl.pallas_call(functools.partial(main_kernel, n), out_shape=(jax.ShapeDty...  42.1 us
    pallas_call x1, Pallas kernels, on_device(): pl.pallas_call(functools.partial(place_kernel, n), out_shape=(jax.ShapeDt...  3.32 us

profile of v2, /device:TPU:18, one launch (start us, length us, event | category | flops | bytes accessed | tf_op | source)
XLA Modules:
  0.0 46.1 jit_solution(10134254434295990404)
XLA Ops:
  0.6 0.0 copy-start
  0.6 42.1 %serve.1 = (bf16[24,2,16,1024]{3,2,1,0:T(8,128)(2,1)S(1)}, bf16[48,2,16,1024]{3,2,1,0:T(8,128)(2,1)S(1)}, bf16[64,1024]{1,0:T(8,128)(2,1)S(1)}) custom-call(s32[5,32]{1,0:T(8,128)} %bitcast.5, s32[16]{0:T(128)} %lens.1, s32[5,32]{1,0:T(8,128)} %bitcast.6, s32[1,16]{1,0:T(1,128)} %bitcast.10, bf16[16,1024]{1,0:T(8,128)(2,1)} %refs_2_.1, ...), custom_call_target="tpu_custom_call" | custom-call | tf_op jit(solution)/shard_map/serve/pallas_call | solution.py:357
  42.7 0.0 copy-done
  42.8 3.3 %place.1 = (bf16[48,2,16,1024]{3,2,1,0:T(8,128)(2,1)}, bf16[64,1024]{1,0:T(8,128)(2,1)}) custom-call(s32[5,32]{1,0:T(8,128)S(1)} %bitcast.7, bf16[48,2,16,1024]{3,2,1,0:T(8,128)(2,1)S(1)} %get-tuple-element.7.resident, bf16[24,2,16,1024]{3,2,1,0:T(8,128)(2,1)S(1)} %get-tuple-element.8.inbound, bf16[64,1024]{1,0:T(8,128)(2,1)S(1)} %get-tuple-element.9.logits_in), custom_call_target="tpu_custom_call" | custom-call | tf_op jit(solution)/shard_map/place/pallas_call | solution.py:398
Async XLA Ops:
  0.6 42.1 %copy-start = (s32[32,5]{0,1:T(8,128)S(1)}, s32[32,5]{0,1:T(8,128)}, u32[]{:S(2)}) copy-start(s32[32,5]{0,1:T(8,128)} %param.18) | copy-start | bytes 1924

commit v3 on v2

--- a/solution.py
+++ b/solution.py
@@ -11,7 +11,7 @@
 PAGES = 3
 GROUP = 8
 COLS = 512
-EARLY = 2
+EARLY = 1
 F32 = jnp.float32
 BF16 = jnp.bfloat16
 MESH = pl.DeviceIdType.MESH
@@ -131,17 +131,6 @@
         msg32[:, 3 * heads + c, :] = sent_len
     msg[...] = msg32[...].astype(BF16)
 
-    def find(r, bases):
-        ahead = rec[2, r] - me
-        ahead = jnp.where(ahead < 0, ahead + n, ahead)
-        ahead = jnp.where(rec[1, r] == me, ahead, -1)
-        first = rec[4, r] - homes
-        return tuple(jnp.where(ahead == s, first, b) for s, b in enumerate(bases))
-
-    bases = lax.fori_loop(0, rows, find, tuple(jnp.int32(0) for _ in range(n)))
-    for s in range(n):
-        base_s[s] = jnp.clip(bases[s], 0, held.shape[0] - PAGES)
-
     pl.semaphore_wait(barrier, n)
     msgs, pages, reps = [], [], []
     for s in range(1, n):
@@ -155,6 +144,17 @@
         reps.append(pltpu.make_async_remote_copy(
             rep.at[s], rep_in.at[s], rep_ss.at[s], rep_rs.at[s],
             device_id=peer(s), device_id_type=MESH))
+    def find(r, bases):
+        ahead = rec[2, r] - me
+        ahead = jnp.where(ahead < 0, ahead + n, ahead)
+        ahead = jnp.where(rec[1, r] == me, ahead, -1)
+        first = rec[4, r] - homes
+        return tuple(jnp.where(ahead == s, first, b) for s, b in enumerate(bases))
+
+    bases = lax.fori_loop(0, rows, find, tuple(jnp.int32(0) for _ in range(n)))
+    for s in range(n):
+        base_s[s] = jnp.clip(bases[s], 0, held.shape[0] - PAGES)
+
     load_held.wait()
     order = sorted(range(1, n), key=lambda s: abs(2 * s - n))
     for k, s in enumerate(order + [0]):

time: 46.3 us -> 46.2 us (level)
  no operation moved by 1% of the time
where the time goes in v3:
time: 46.2 us; the launch traced here: 45.6 us
  Pallas kernels  45 us (97%)
  between operations  0.66 us (1%)
    pallas_call x1, Pallas kernels, on_device(): pl.pallas_call(functools.partial(main_kernel, n), out_shape=(jax.ShapeDty...  42 us
    pallas_call x1, Pallas kernels, on_device(): pl.pallas_call(functools.partial(place_kernel, n), out_shape=(jax.ShapeDt...  3.01 us

profile of v3, /device:TPU:18, one launch (start us, length us, event | category | flops | bytes accessed | tf_op | source)
XLA Modules:
  0.0 45.6 jit_solution(6435790507112104825)
XLA Ops:
  0.6 0.0 copy-start
  0.6 42.0 %serve.1 = (bf16[24,2,16,1024]{3,2,1,0:T(8,128)(2,1)S(1)}, bf16[48,2,16,1024]{3,2,1,0:T(8,128)(2,1)S(1)}, bf16[64,1024]{1,0:T(8,128)(2,1)S(1)}) custom-call(s32[5,32]{1,0:T(8,128)} %bitcast.5, s32[16]{0:T(128)} %lens.1, s32[5,32]{1,0:T(8,128)} %bitcast.6, s32[1,16]{1,0:T(1,128)} %bitcast.10, bf16[16,1024]{1,0:T(8,128)(2,1)} %refs_2_.1, ...), custom_call_target="tpu_custom_call" | custom-call | tf_op jit(solution)/shard_map/serve/pallas_call | solution.py:357
  42.6 0.0 copy-done
  42.6 3.0 %place.1 = (bf16[48,2,16,1024]{3,2,1,0:T(8,128)(2,1)}, bf16[64,1024]{1,0:T(8,128)(2,1)}) custom-call(s32[5,32]{1,0:T(8,128)S(1)} %bitcast.7, bf16[48,2,16,1024]{3,2,1,0:T(8,128)(2,1)S(1)} %get-tuple-element.7.resident, bf16[24,2,16,1024]{3,2,1,0:T(8,128)(2,1)S(1)} %get-tuple-element.8.inbound, bf16[64,1024]{1,0:T(8,128)(2,1)S(1)} %get-tuple-element.9.logits_in), custom_call_target="tpu_custom_call" | custom-call | tf_op jit(solution)/shard_map/place/pallas_call | solution.py:398
Async XLA Ops:
  0.6 42.0 %copy-start = (s32[32,5]{0,1:T(8,128)S(1)}, s32[32,5]{0,1:T(8,128)}, u32[]{:S(2)}) copy-start(s32[32,5]{0,1:T(8,128)} %param.18) | copy-start | bytes 1924
